TPU v7x, 512 devices: a whole 4x4x16 slice. The times are simulated.
512 devices in a mesh: member: 16 (over z_hi, y, core), tensor: 32 (over z_lo, x).
Axes of the slice: x: 4, y: 4, z: 16 (z_hi: 2, z_lo: 8; z = z_hi * 8 + z_lo), core: 2. Of those that a mesh axis runs over, the one named last changes fastest.
Arguments:
- layer_input: bfloat16 [16, 4096, 8192], P('member', 'tensor'), may hold values from -6 to 6
- value_grads: bfloat16 [16, 4096, 1024], P('member', 'tensor'), may hold values from -6 to 6
- value_weight: bfloat16 [8192, 1024], P('tensor', 'member'), may hold values from -0.0625 to 0.0625
- adapter_down: bfloat16 [16, 8192, 64], P('member', 'tensor'), may hold values from -0.0625 to 0.0625
- adapter_up: bfloat16 [16, 64, 1024], P('member'), may hold values from -0.1875 to 0.1875
- norm_gain: float32 [8192], replicated, may hold values from 0.1 to 1.9
Outputs:
- input_grads: bfloat16 [16, 4096, 8192], P('member', 'tensor')
- down_grads: float32 [16, 8192, 64], P('member', 'tensor')
- up_grads: float32 [16, 64, 1024], P('member', None, 'tensor')
All inputs are finite; a program needn't handle non-finite values.
Results may differ from a plain program's by a relative error of at most 0.0054.
Values may be sent and summed in bfloat16 or wider, within the bound.
A program may use at most 64 MiB of HBM per device.

v0:
```python
import math

import jax
import jax.numpy as jnp
from jax import lax
from jax.sharding import PartitionSpec as P

adapter_scale = 4.0
gradient_scale = 1.0
norm_eps = 1e-05


def per_device(layer_input, value_grads, value_weight, adapter_down, adapter_up, norm_gain):
    member_token_rows = layer_input.shape[1] * lax.axis_size("tensor")
    scaling_multiplier = gradient_scale / math.sqrt(member_token_rows)
    own_input = layer_input[0]
    own_grads = value_grads[0]
    up_weight = adapter_up[0]
    down_slice = adapter_down[0]
    weight_rows = lax.all_gather(value_weight, "member", axis=1, tiled=True)
    grads_all = lax.all_gather(own_grads, "tensor", axis=0, tiled=True)
    widened = own_input.astype(jnp.float32)
    inverse_rms = lax.rsqrt(jnp.mean(widened * widened, axis=-1, keepdims=True) + norm_eps)
    normed = widened * inverse_rms
    scaled = (normed * norm_gain).astype(jnp.bfloat16)
    lowrank_own = jnp.dot(own_grads, up_weight.T, preferred_element_type=jnp.float32).astype(
        jnp.bfloat16
    )
    lowrank_all = lax.all_gather(lowrank_own, "tensor", axis=0, tiled=True)
    frozen_product = jnp.dot(grads_all, weight_rows.T, preferred_element_type=jnp.float32)
    adapter_product = jnp.dot(lowrank_all, down_slice.T, preferred_element_type=jnp.float32)
    slice_gradient = (frozen_product + adapter_scale * adapter_product).astype(jnp.bfloat16)
    feature_gradient = lax.all_to_all(
        slice_gradient, "tensor", split_axis=0, concat_axis=1, tiled=True
    )
    gained = norm_gain * feature_gradient.astype(jnp.float32)
    center = jnp.mean(gained * normed, axis=-1, keepdims=True)
    input_grads = (inverse_rms * (gained - normed * center)).astype(jnp.bfloat16)
    down_full = lax.all_gather(down_slice, "tensor", axis=0, tiled=True)
    lowrank_in = jnp.dot(scaled, down_full, preferred_element_type=jnp.float32).astype(jnp.bfloat16)
    up_term = jnp.dot(lowrank_in.T, own_grads, preferred_element_type=jnp.float32)
    up_grads = scaling_multiplier * lax.psum_scatter(
        up_term, "tensor", scatter_dimension=1, tiled=True
    )
    down_sum = lax.psum_scatter(
        jnp.dot(scaled.T, lowrank_own, preferred_element_type=jnp.float32),
        "tensor",
        scatter_dimension=0,
        tiled=True,
    )
    down_grads = scaling_multiplier * down_sum
    return (input_grads[None], down_grads[None], up_grads[None])


def solution(mesh):
    return jax.shard_map(
        per_device,
        mesh=mesh,
        in_specs=(
            P("member", "tensor", None),
            P("member", "tensor", None),
            P("tensor", "member"),
            P("member", "tensor", None),
            P("member", None, None),
            P(),
        ),
        out_specs=(
            P("member", "tensor", None),
            P("member", "tensor", None),
            P("member", None, "tensor"),
        ),
        check_vma=False,
    )
```

profile of v0, /device:TPU:8, one launch (start us, length us, event | category | flops | bytes accessed | tf_op | source)
XLA Modules:
  0.0 956.2 jit_solution(2324736798573502716)
XLA Ops:
  7.2 0.0 copy-start
  7.2 0.0 all-gather.5.cloned.1.call-start
  7.2 0.7 all-gather.5.cloned.1.call-update
  7.9 0.2 copy-done
  8.1 1.2 convolution_convert_fusion.1
  9.2 41.7 %all_gather.13 = bf16[256,1024]{0,1:T(8,128)(2,1)S(1)} all-gather(bf16[256,64]{0,1:T(8,128)(2,1)} %param.8), channel_id=1, replica_groups=mesh['member'=16,'tensor'=32] {'member'}, dimensions={1}, use_global_device_ids=true | all-gather | bytes 557056 | tf_op jit(solution)/shard_map/all_gather | solution.py:20
  50.9 122.0 %all_gather.14 = bf16[4096,64]{0,1:T(8,128)(2,1)S(1)} all-gather(bf16[128,64]{0,1:T(8,128)(2,1)S(1)} %convolution_convert_fusion.1), channel_id=1, replica_groups=mesh['member'=16,'tensor'=32] {'tensor'}, dimensions={0}, use_global_device_ids=true | all-gather | bytes 540672 | tf_op jit(solution)/shard_map/all_gather | solution.py:29
  172.9 79.0 %all-gather.5.cloned.1.call-done = bf16[1,4096,1024]{2,1,0:T(8,128)(2,1)} async-done(((bf16[1,128,1024]{2,1,0:T(8,128)(2,1)}), bf16[1,4096,1024]{2,1,0:T(8,128)(2,1)}) %all-gather.5.cloned.1.call-update) | async-done | bytes 8388624 | tf_op jit(solution)/shard_map/all_gather | solution.py:21
  251.9 5.9 fusion
  257.9 0.0 copy-start.1
  257.9 2.1 fusion.3
  260.0 11.4 %all-to-all-start = ((bf16[32,128,256]{2,1,0:T(8,128)(2,1)}), bf16[32,128,256]{2,1,0:T(8,128)(2,1)}, u32[]{:S(2)}, u32[]{:S(2)}) async-start(bf16[32,128,256]{2,1,0:T(8,128)(2,1)} %bitcast.52), calls=%async_computation | async-start | bytes 4194304 | tf_op jit(solution)/shard_map/all_to_all | solution.py:33
  271.3 0.0 all-gather.7.cloned.1.call-start
  271.4 0.7 all-gather.7.cloned.1.call-update
  272.1 0.0 reduce-scatter.5.cloned.1.call-start
  272.2 0.5 fusion.7
  272.7 183.0 %all-gather.7.cloned.1.call-done = bf16[1,8192,64]{1,2,0:T(8,128)(2,1)} async-done(((bf16[1,256,64]{1,2,0:T(8,128)(2,1)}), bf16[1,8192,64]{1,2,0:T(8,128)(2,1)}) %all-gather.7.cloned.1.call-update) | async-done | bytes 1048592 | tf_op jit(solution)/shard_map/all_gather | solution.py:39
  455.7 3.1 fusion.10
  458.8 0.0 reduce-scatter.5.cloned.1.call-update
  458.8 0.2 reduce-scatter.3.cloned.1.call-start
  459.0 2.2 fusion.15
  461.2 0.0 reduce-scatter.3.cloned.1.call-update
  461.2 2.6 copy.11
  463.8 227.9 %reduce-scatter.5.cloned.1.call-done = f32[64,32]{0,1:T(8,128)} async-done(((f32[64,1024]{0,1:T(8,128)}), f32[64,32]{0,1:T(8,128)}) %reduce-scatter.5.cloned.1.call-update) | async-done | bytes 8208 | tf_op jit(solution)/shard_map/reduce_scatter | solution.py:42
  691.7 1.3 multiply_bitcast_fusion.1
  693.1 235.6 %reduce-scatter.3.cloned.1.call-done = f32[256,64]{0,1:T(8,128)} async-done(((f32[8192,64]{0,1:T(8,128)}), f32[256,64]{0,1:T(8,128)}) %reduce-scatter.3.cloned.1.call-update) | async-done | bytes 65552 | tf_op jit(solution)/shard_map/reduce_scatter | solution.py:45
  928.7 1.5 multiply_bitcast_fusion
  930.2 2.1 convert_bitcast_fusion
  932.3 4.4 copy.9
  936.7 5.0 reshape.94
  941.6 5.7 fusion.6
  947.3 2.3 multiply_convert_fusion
  (13 shorter events, 0.0 us)
Async XLA Ops:
  7.2 0.9 copy-start
  7.2 244.8 %all-gather.5.cloned.1.call-start = ((), (), s32[]{:S(2)}) async-start(), calls=%async_computation.5 | async-start | bytes 8650752 | tf_op jit(solution)/shard_map/all_gather | solution.py:21
  172.9 84.9 %copy-start.5 = (bf16[1,256,64]{1,2,0:T(8,128)(2,1)S(1)}, bf16[1,256,64]{1,2,0:T(8,128)(2,1)}, u32[]{:S(2)}) copy-start(bf16[1,256,64]{1,2,0:T(8,128)(2,1)} %param.9) | copy-start | bytes 98308
  257.9 14.3 %copy-start.1 = (bf16[1,128,8192]{2,1,0:T(8,128)(2,1)S(1)}, bf16[1,128,8192]{2,1,0:T(8,128)(2,1)}, u32[]{:S(2)}) copy-start(bf16[1,128,8192]{2,1,0:T(8,128)(2,1)} %param.6) | copy-start | bytes 6291460
  259.9 195.7 %copy-start.3 = (bf16[1,128,1024]{2,1,0:T(8,128)(2,1)S(1)}, bf16[1,128,1024]{2,1,0:T(8,128)(2,1)}, u32[]{:S(2)}) copy-start(bf16[1,128,1024]{2,1,0:T(8,128)(2,1)} %param.7) | copy-start | bytes 786436
  259.9 195.7 %copy-start.4 = (f32[8192]{0:T(1024)S(1)}, f32[8192]{0:T(1024)}, u32[]{:S(2)}) copy-start(f32[8192]{0:T(1024)} %param.11) | copy-start | bytes 98308
  260.0 670.2 %all-to-all-start = ((bf16[32,128,256]{2,1,0:T(8,128)(2,1)}), bf16[32,128,256]{2,1,0:T(8,128)(2,1)}, u32[]{:S(2)}, u32[]{:S(2)}) async-start(bf16[32,128,256]{2,1,0:T(8,128)(2,1)} %bitcast.52), calls=%async_computation | async-start | bytes 4194304 | tf_op jit(solution)/shard_map/all_to_all | solution.py:33
  271.3 184.3 %all-gather.7.cloned.1.call-start = ((), (), s32[]{:S(2)}) async-start(), calls=%async_computation.6 | async-start | bytes 1081344 | tf_op jit(solution)/shard_map/all_gather | solution.py:39
  272.1 419.6 %reduce-scatter.5.cloned.1.call-start = ((), (), s32[]{:S(2)}) async-start(), calls=%async_computation.4 | async-start | bytes 540672 | tf_op jit(solution)/shard_map/reduce_scatter | solution.py:42
  458.8 469.9 %reduce-scatter.3.cloned.1.call-start = ((), (), s32[]{:S(2)}) async-start(), calls=%async_computation.3 | async-start | bytes 2162688 | tf_op jit(solution)/shard_map/reduce_scatter | solution.py:45
  941.6 5.7 copy-start.2
Sparse Core Ops, SparseCore 0:
  10.1 241.7 all-gather.4
  274.2 181.4 all-gather.6
  458.9 232.7 reduce-scatter.4
  694.6 234.0 reduce-scatter.2
where the time goes:
time: 957 us; the launch traced here: 956 us
  waiting for transfers between devices  727 us (76%)
  blocking collectives  164 us (17%)
  matrix products  14.4 us (2%)
  between operations  13.9 us (1%)
  other arithmetic  13.4 us (1%)
  local copies, waits for them, and re-layouts  12.1 us (1%)
  starting transfers between devices  11.7 us (1%)
    reduce_scatter x1, waiting for transfers between devices, per_device(): lax.psum_scatter(jnp.dot(scaled.T, lowrank_own, preferred_element_type=jn...  236 us
    reduce_scatter x1, waiting for transfers between devices, per_device(): lax.psum_scatter(up_term, 'tensor', scatter_dimension=1, tiled=True)  228 us
    all_gather x1, waiting for transfers between devices, per_device(): down_full = lax.all_gather(down_slice, 'tensor', axis=0, tiled=True)  183 us
    all_gather x1, blocking collectives, per_device(): lowrank_all = lax.all_gather(lowrank_own, 'tensor', axis=0, tiled=True)  122 us
    all_gather x1, waiting for transfers between devices, per_device(): grads_all = lax.all_gather(own_grads, 'tensor', axis=0, tiled=True)  79 us
    all_gather x1, blocking collectives, per_device(): weight_rows = lax.all_gather(value_weight, 'member', axis=1, tiled=True)  41.7 us
  transfers between devices with their start and end apart: 5, of which 4 were waited for; matrix products, arithmetic and copies ran while one was open for 1% of the time, Pallas kernels for 0%

commit v1 on v0

v1 whole, which is shorter than its diff:
```python
import functools
import math

import jax
import jax.numpy as jnp
from jax import lax
from jax.experimental import pallas as pl
from jax.experimental.pallas import tpu as pltpu
from jax.sharding import PartitionSpec as P

adapter_scale = 4.0
gradient_scale = 1.0
norm_eps = 1e-05

F32 = jnp.float32
BF16 = jnp.bfloat16
MESH = pl.DeviceIdType.MESH
ZL, ZH, NX, NY = 8, 2, 4, 4
NZ = ZL * ZH
D = 8192
KV = 1024
R = 64
T = 128
B = 256
NN = (((1,), (0,)), ((), ()))
NT = (((1,), (1,)), ((), ()))
TN = (((0,), (0,)), ((), ()))


def dot(a, b, dims):
    return lax.dot_general(a, b, dims, preferred_element_type=F32)


def mod(a, n):
    return lax.rem(a + 4 * n, n)


def main_kernel(
    x_hbm, grads, w_in, d_in, up, gain,
    fg, down_out, up_out,
    xv, scaled, buf, dbuf, tok, lr4, res, inv,
    part, part_in, summed, chain, lin, upart, upart_in, usum, uin,
    s_loc, s_w2, s_g, s_z, s_y1, s_y2, s_sib, s_d, s_p, s_c, s_res, s_own, s_u, s_uz,
):
    m = lax.axis_index("member")
    t = lax.axis_index("tensor")
    zh, y, c = m // 8, (m // 2) % 4, m % 2
    zl, xx = t // 4, t % 4
    z = zh * ZL + zl
    par, xs = xx % 2, xx // 2
    sib_c = 1 - c

    def dev(z_, y_, x_, c_):
        return ((z_ // ZL) * 8 + y_ * 2 + c_, (z_ % ZL) * 4 + x_)

    zp, zm = dev(mod(z + 1, NZ), y, xx, c), dev(mod(z - 1, NZ), y, xx, c)
    yp, ym = dev(z, mod(y + 1, NY), xx, c), dev(z, mod(y - 1, NY), xx, c)
    sib = dev(z, y, xx, sib_c)

    def xdev(d):
        return dev(z, y, mod(xx + d, NX), c)

    def remote(src, dst, sems, idx, target):
        return pltpu.make_async_remote_copy(
            src_ref=src, dst_ref=dst, send_sem=sems.at[(0,) + idx],
            recv_sem=sems.at[(1,) + idx], device_id=target, device_id_type=MESH,
        )

    sends = []

    def start(src, dst, sems, idx, target):
        cp = remote(src, dst, sems, idx, target)
        cp.start()
        sends.append(cp)

    def arrived(ref, sems, idx):
        remote(ref, ref, sems, idx, sib).wait_recv()

    load_x = pltpu.make_async_copy(x_hbm, xv, s_loc)
    load_x.start()

    barrier = pltpu.get_barrier_semaphore()
    for peer in (zp, zm, yp, ym, xdev(1), xdev(2), xdev(3), sib):
        pl.semaphore_signal(barrier, inc=1, device_id=peer, device_id_type=MESH)

    eye = (
        lax.broadcasted_iota(jnp.int32, (R, R), 0) == lax.broadcasted_iota(jnp.int32, (R, R), 1)
    ).astype(BF16)

    def piece(zsrc, parts, ysrc, csrc):
        return buf.at[parts, zsrc % ZL, zsrc // ZL, ysrc, csrc]

    buf[xs, zl, zh, y, c] = dot(eye, w_in[...], NT).astype(BF16)
    dt_own = dot(eye, d_in[...], NT).astype(BF16)
    buf[2, zl, zh, y, c] = dt_own
    dbuf[zl, xx] = dt_own
    pl.semaphore_wait(barrier, 8)

    start(piece(z, xs, y, c), piece(z, xs, y, c), s_w2, (), xdev(2))
    tok[0:T] = grads[...]
    start(grads.at[0:64], tok.at[128:192], s_g, (0,), xdev(1))
    start(grads.at[64:128], tok.at[192:256], s_g, (1,), xdev(3))

    lr_own = dot(grads[...], up[...], NT).astype(BF16)
    lr_t = dot(up[...], grads[...], NT).astype(BF16)
    lr4[0:T] = lr_own * adapter_scale

    load_x.wait()

    def square(i, acc):
        v = xv[:, pl.ds(pl.multiple_of(i * B, B), B)].astype(F32)
        return acc + v * v

    total = lax.fori_loop(0, 32, square, jnp.zeros((T, B), F32))
    inv[...] = lax.rsqrt(jnp.sum(total, axis=1, keepdims=True) / D + norm_eps)

    arrived(piece(z, 1 - xs, y, c), s_w2, ())

    def source(q):
        steps = (q + 1) // 2
        return mod(z - steps, NZ) if q % 2 else mod(z + steps, NZ)

    def of_step(s):
        return [0] if s == 0 else ([15] if s == 8 else [2 * s - 1, 2 * s])

    def z_parts(s, direction):
        return pl.ds(0, 3) if s < 8 else (0 if direction == 0 else 1)

    def z_send(s):
        up_src, down_src = mod(z - s + 1, NZ), mod(z + s - 1, NZ)
        a = piece(up_src, z_parts(s, 0), y, c)
        b = piece(down_src, z_parts(s, 1), y, c)
        start(a, a, s_z, (0, s), zp)
        start(b, b, s_z, (1, s), zm)

    def z_wait(s):
        arrived(piece(mod(z - s, NZ), z_parts(s, 0), y, c), s_z, (0, s))
        arrived(piece(mod(z + s, NZ), z_parts(s, 1), y, c), s_z, (1, s))

    both = pl.ds(0, 2)

    def y_send(q):
        src = piece(source(q), both, y, c)
        start(src, src, s_y1, (0, q), yp)
        start(src, src, s_y1, (1, q), ym)

    def y_relay(q):
        below, above = mod(y - 1, NY), mod(y + 1, NY)
        arrived(piece(source(q), both, below, c), s_y1, (0, q))
        src = piece(source(q), 0, below, c)
        start(src, src, s_y2, (0, q), yp)
        arrived(piece(source(q), both, above, c), s_y1, (1, q))
        src = piece(source(q), 1, above, c)
        start(src, src, s_y2, (1, q), ym)

    def y_done(q):
        far = mod(y + 2, NY)
        arrived(piece(source(q), 0, far, c), s_y2, (0, q))
        arrived(piece(source(q), 1, far, c), s_y2, (1, q))
        src = piece(source(q), both, slice(None), c)
        start(src, src, s_sib, (q,), sib)

    def sib_done(q):
        arrived(piece(source(q), both, slice(None), sib_c), s_sib, (q,))

    def in_line(s, direction):
        return zl >= s if direction == 0 else zl + s < ZL

    def d_send(s):
        for direction in (0, 1) if s else (0,):
            row = zl - s if direction == 0 else zl + s

            def go(row=row):
                src = buf.at[2, row, zh, y, c]
                if s:
                    dbuf[row, xx] = src[...]
                for d in (1, 2, 3):
                    remote(src, dbuf.at[row, xx], s_d, (d, row), xdev(d)).start()

            pl.when(in_line(s, direction))(go)

    def d_done(s):
        for direction in (0, 1) if s else (0,):
            row = zl - s if direction == 0 else zl + s

            def go(row=row):
                for d in (1, 2, 3):
                    remote(dbuf.at[row, xx], dbuf.at[row, mod(xx - d, NX)], s_d, (d, row), sib).wait()

                def add(i, acc):
                    return acc + dot(scaled[row * 4 + i], dbuf[row, i], NT)

                lin[...] += lax.fori_loop(0, 4, add, jnp.zeros((T, R), F32))

            pl.when(in_line(s, direction))(go)

    def rows_of(j):
        if j == 8:
            return [(True, zl)]
        return [(zl + 8 - j < ZL, zl + 8 - j), (zl - 8 + j >= 0, zl - 8 + j)]

    def p_send(j):
        for ok, row in rows_of(j):

            def go(row=row):
                def one(i, carry):
                    part[i, row] = dot(lr_t, scaled[row * 4 + i], NN).astype(BF16)
                    return carry

                lax.fori_loop(0, 4, one, 0)
                for d in (1, 2, 3):
                    remote(
                        part.at[mod(xx + d, NX), row], part_in.at[d, row], s_p, (d, row), xdev(d)
                    ).start()

            if ok is True:
                go()
            else:
                pl.when(ok)(go)

    def p_done(j):
        for ok, row in rows_of(j):

            def go(row=row):
                acc = part[xx, row].astype(F32)
                for d in (1, 2, 3):
                    remote(
                        part.at[mod(xx + d, NX), row], part_in.at[d, row], s_p, (d, row), sib
                    ).wait()
                    acc += part_in[d, row].astype(F32)
                summed[row] = acc

            if ok is True:
                go()
            else:
                pl.when(ok)(go)

    def c_step(j):
        for direction, place, peer, row in (
            (0, zl, zp, zl + 8 - j), (1, 7 - zl, zm, zl - 8 + j)
        ):
            if j <= 7:

                def first(direction=direction, peer=peer, row=row):
                    remote(
                        summed.at[row], chain.at[direction, j], s_c, (direction, j), peer
                    ).start()

                pl.when(place == 0)(first)
                if j >= 2:

                    def later(direction=direction, peer=peer, row=row):
                        arrived(chain.at[direction, j - 1], s_c, (direction, j - 1))
                        chain[direction, j - 1] += summed[row]
                        remote(
                            chain.at[direction, j - 1], chain.at[direction, j], s_c,
                            (direction, j), peer,
                        ).start()

                    pl.when((place >= 1) & (place <= j - 1))(later)

    def c_last():
        down_out[...] = summed[zl]
        for direction, place in ((0, zl), (1, 7 - zl)):

            def go(direction=direction):
                arrived(chain.at[direction, 7], s_c, (direction, 7))
                down_out[...] += chain[direction, 7]

            pl.when(place >= 1)(go)

    def block(row):
        def one(i, carry):
            w = buf[i, row].reshape(KV, B)
            acc = dot(tok[...], w, NN) + dot(lr4[...], dbuf[row, par + 2 * i], NN)
            res[row, i] = acc.astype(BF16)
            return carry

        lax.fori_loop(0, 2, one, 0)
        remote(
            res.at[row, :, 128:192], fg.at[row, :, par, 0:64], s_res, (0, row), xdev(3)
        ).start()
        remote(
            res.at[row, :, 192:256], fg.at[row, :, par, 64:128], s_res, (1, row), xdev(1)
        ).start()
        pltpu.make_async_copy(res.at[row, :, 0:128], fg.at[row, :, par], s_own.at[row]).start()

    def finished(s):
        if s < 4:
            return []
        if s == 4:
            return [mod(zl + 4, ZL)]
        if s == 8:
            return [zl]
        return [mod(zl + s, ZL), mod(zl - s, ZL)]

    def pack_up():
        lb = lin[...].astype(BF16)
        term = dot(grads[...], lb, TN)
        upart[...] = term.reshape(ZL, NX, 32, R).swapaxes(0, 1).astype(BF16)
        for d in (1, 2, 3):
            start(upart.at[mod(xx + d, NX)], upart_in.at[d], s_u, (d,), xdev(d))

    def up_over_z():
        acc = upart[xx].astype(F32)
        for d in (1, 2, 3):
            arrived(upart_in.at[d], s_u, (d,))
            acc += upart_in[d].astype(F32)
        usum[...] = acc
        for d in range(1, 8):
            row = mod(zl + d, ZL)
            start(usum.at[row], uin.at[d], s_uz, (d,), dev(zh * ZL + row, y, xx, c))

    def up_last():
        acc = usum[zl]
        for d in range(1, 8):
            arrived(uin.at[d], s_uz, (d,))
            acc += uin[d]
        up_out[...] = acc

    def make_scaled(i, carry):
        v = xv[:, pl.ds(pl.multiple_of(i * B, B), B)].astype(F32)
        scaled[i] = (v * inv[...] * gain[pl.ds(i, 1), :]).astype(BF16)
        return carry

    lin[...] = jnp.zeros_like(lin)
    for s in range(0, 12):
        if 1 <= s <= 8:
            z_wait(s)
        if s <= 7:
            z_send(s + 1)
        if s <= 8:
            for q in of_step(s):
                y_send(q)
        if s <= 7:
            d_send(s)
        if s == 0:
            lax.fori_loop(0, 32, make_scaled, 0)
        if 1 <= s <= 8:
            p_send(s)
        if 0 <= s - 1 <= 8:
            for q in of_step(s - 1):
                y_relay(q)
        if s == 1:
            arrived(tok.at[128:192], s_g, (0,))
            arrived(tok.at[192:256], s_g, (1,))
            lr4[T:] = dot(tok[T:], up[...], NT).astype(BF16) * adapter_scale
        if 0 <= s - 2 <= 7:
            p_done(s - 1)
        if 1 <= s - 2 <= 7:
            c_step(s - 2)
        if 0 <= s - 1 <= 7:
            d_done(s - 1)
        if s == 8:
            pack_up()
        if s == 10:
            up_over_z()
        if 0 <= s - 2 <= 8:
            for q in of_step(s - 2):
                y_done(q)
        if 0 <= s - 3 <= 8:
            for q in of_step(s - 3):
                sib_done(q)
            for row in finished(s - 3):
                block(row)

    c_last()
    up_last()
    for row in range(ZL):
        pltpu.make_async_copy(res.at[row, :, 0:128], fg.at[row, :, par], s_own.at[row]).wait()
        remote(
            res.at[row, :, 128:192], fg.at[row, :, 1 - par, 0:64], s_res, (0, row), sib
        ).wait()
        remote(
            res.at[row, :, 192:256], fg.at[row, :, 1 - par, 64:128], s_res, (1, row), sib
        ).wait()
    for j in range(1, 8):
        for direction, place in ((0, zl), (1, 7 - zl)):

            def go(direction=direction, j=j):
                remote(summed.at[0], chain.at[direction, j], s_c, (direction, j), sib).wait_send()

            pl.when(place <= j - 1)(go)
    for cp in sends:
        cp.wait_send()


def exchange(x, grads, w, d, up, gain):
    sem = pltpu.SemaphoreType.DMA
    vmem = pl.BlockSpec(memory_space=pltpu.VMEM)
    hbm = pl.BlockSpec(memory_space=pl.ANY)
    return pl.pallas_call(
        main_kernel,
        out_shape=(
            jax.ShapeDtypeStruct((ZL, 2, 2, T, B), BF16),
            jax.ShapeDtypeStruct((R, B), F32),
            jax.ShapeDtypeStruct((32, R), F32),
        ),
        in_specs=[hbm, vmem, vmem, vmem, vmem, vmem],
        out_specs=(hbm, vmem, vmem),
        scratch_shapes=[
            pltpu.VMEM((T, D), BF16),
            pltpu.VMEM((32, T, B), BF16),
            pltpu.VMEM((3, ZL, ZH, NY, 2, R, B), BF16),
            pltpu.VMEM((ZL, NX, R, B), BF16),
            pltpu.VMEM((2 * T, KV), BF16),
            pltpu.VMEM((2 * T, R), BF16),
            pltpu.VMEM((ZL, 2, 2 * T, B), BF16),
            pltpu.VMEM((T, 1), F32),
            pltpu.VMEM((NX, ZL, R, B), BF16),
            pltpu.VMEM((NX, ZL, R, B), BF16),
            pltpu.VMEM((ZL, R, B), F32),
            pltpu.VMEM((2, 8, R, B), F32),
            pltpu.VMEM((T, R), F32),
            pltpu.VMEM((NX, ZL, 32, R), BF16),
            pltpu.VMEM((NX, ZL, 32, R), BF16),
            pltpu.VMEM((ZL, 32, R), F32),
            pltpu.VMEM((ZL, 32, R), F32),
            sem,
            sem((2,)),
            sem((2, 2)),
            sem((2, 2, 9)),
            sem((2, 2, 16)),
            sem((2, 2, 16)),
            sem((2, 16)),
            sem((2, 4, 8)),
            sem((2, 4, 8)),
            sem((2, 2, 8)),
            sem((2, 2, 8)),
            sem((8,)),
            sem((2, 4)),
            sem((2, 8)),
        ],
        compiler_params=pltpu.CompilerParams(
            collective_id=1, has_side_effects=True, vmem_limit_bytes=50 << 20
        ),
        name="exchange",
    )(x, grads, w, d, up, gain)


def finish_kernel(x, fg, gain, out):
    rows = x.shape[0]
    squares = jnp.zeros((rows, B), F32)
    products = jnp.zeros((rows, B), F32)
    for i in range(32):
        v = x[:, i * B:(i + 1) * B].astype(F32)
        g = fg[i // 4, (i % 4) // 2, i % 2].astype(F32) * gain[i:i + 1, :]
        squares += v * v
        products += v * g
    inv = lax.rsqrt(jnp.sum(squares, axis=1, keepdims=True) / D + norm_eps)
    slope = inv * inv * (jnp.sum(products, axis=1, keepdims=True) / D)
    for i in range(32):
        v = x[:, i * B:(i + 1) * B].astype(F32)
        g = fg[i // 4, (i % 4) // 2, i % 2].astype(F32) * gain[i:i + 1, :]
        out[:, i * B:(i + 1) * B] = (inv * (g - v * slope)).astype(BF16)


def finish(x, fg, gain):
    rows = 32
    return pl.pallas_call(
        finish_kernel,
        grid=(T // rows,),
        out_shape=jax.ShapeDtypeStruct((T, D), BF16),
        in_specs=[
            pl.BlockSpec((rows, D), lambda i: (i, 0)),
            pl.BlockSpec((ZL, 2, 2, rows, B), lambda i: (0, 0, 0, i, 0)),
            pl.BlockSpec((32, B), lambda i: (0, 0)),
        ],
        out_specs=pl.BlockSpec((rows, D), lambda i: (i, 0)),
        compiler_params=pltpu.CompilerParams(vmem_limit_bytes=32 << 20),
        name="finish",
    )(x, fg, gain)


def per_device(layer_input, value_grads, value_weight, adapter_down, adapter_up, norm_gain):
    scaling = gradient_scale / math.sqrt(layer_input.shape[1] * lax.axis_size("tensor"))
    gain = norm_gain.reshape(32, B)
    fg, down_t, up_t = exchange(
        layer_input[0], value_grads[0], value_weight, adapter_down[0], adapter_up[0], gain
    )
    input_grads = finish(layer_input[0], fg, gain)
    return (input_grads[None], (scaling * down_t.T)[None], (scaling * up_t.T)[None])


def solution(mesh):
    return jax.shard_map(
        per_device,
        mesh=mesh,
        in_specs=(
            P("member", "tensor", None),
            P("member", "tensor", None),
            P("tensor", "member"),
            P("member", "tensor", None),
            P("member", None, None),
            P(),
        ),
        out_specs=(
            P("member", "tensor", None),
            P("member", "tensor", None),
            P("member", None, "tensor"),
        ),
        check_vma=False,
    )
```

time: 957 us -> 82.1 us (0.09)
  the two profiles are of different devices: /device:TPU:8 before, /device:TPU:1 now
where the time goes in v1:
time: 82.1 us; the launch traced here: 81.8 us
  Pallas kernels  75.4 us (92%)
  local copies, waits for them, and re-layouts  4.52 us (6%)
  other arithmetic  1.24 us (2%)
    pallas_call x1, Pallas kernels, exchange(): pl.pallas_call(main_kernel, out_shape=(jax.ShapeDtypeStruct((ZL, 2, 2, T,...  72.3 us
    unnamed x8, local copies, waits for them, and re-layouts  3.61 us
    pallas_call x1, Pallas kernels, finish(): pl.pallas_call(finish_kernel, grid=(T // rows,), out_shape=jax.ShapeDtype...  3.09 us

profile of v1, /device:TPU:1, one launch (start us, length us, event | category | flops | bytes accessed | tf_op | source)
XLA Modules:
  0.0 81.8 jit_solution(3484169289555507567)
XLA Ops:
  0.6 0.0 copy-start
  0.6 0.9 %reshape.9.gain = f32[32,256]{1,0:T(8,128)S(1)} reshape(f32[8192]{0:T(1024)} %param.11) | data formatting | bytes 65536 | tf_op jit(solution)/shard_map/reshape | solution.py:477
  1.6 0.9 %copy.10.w_in = bf16[256,64]{1,0:T(8,128)(2,1)S(1)} copy(bf16[256,64]{0,1:T(8,128)(2,1)} %param.8) | data formatting | bytes 65536 | tf_op args[2]
  2.4 0.9 %copy.9 = bf16[1,256,64]{2,1,0:T(8,128)(2,1)S(1)} copy(bf16[1,256,64]{1,2,0:T(8,128)(2,1)} %param.9) | data formatting | bytes 65536 | tf_op args[3]
  3.3 0.0 copy-start.1
  3.3 0.9 %copy-done.1 = bf16[1,128,1024]{2,1,0:T(8,128)(2,1)S(1)} copy-done((bf16[1,128,1024]{2,1,0:T(8,128)(2,1)S(1)}, bf16[1,128,1024]{2,1,0:T(8,128)(2,1)}, u32[]{:S(2)}) %copy-start.1) | copy-done | bytes 262168
  4.3 0.0 copy-start.2
  4.3 0.9 %copy-done.2 = bf16[1,64,1024]{2,1,0:T(8,128)(2,1)S(1)} copy-done((bf16[1,64,1024]{2,1,0:T(8,128)(2,1)S(1)}, bf16[1,64,1024]{2,1,0:T(8,128)(2,1)}, u32[]{:S(2)}) %copy-start.2) | copy-done | bytes 131096
  5.2 72.3 %exchange.1 = (bf16[8,2,2,128,256]{4,3,2,1,0:T(8,128)(2,1)S(1)}, f32[64,256]{1,0:T(8,128)S(1)}, f32[32,64]{1,0:T(8,128)S(1)}) custom-call(bf16[128,8192]{1,0:T(8,128)(2,1)} %bitcast.13, bf16[128,1024]{1,0:T(8,128)(2,1)S(1)} %bitcast.15, bf16[256,64]{1,0:T(8,128)(2,1)S(1)} %copy.10.w_in, bf16[256,64]{1,0:T(8,128)(2,1)S(1)} %bitcast.16, ...), custom_call_target="tpu_custom_call" | custom-call | tf_op jit(solution)/shard_map/exchange/pallas_call | solution.py:392
  77.5 0.0 copy-done
  77.5 3.1 %finish.1 = bf16[128,8192]{1,0:T(8,128)(2,1)} custom-call(bf16[128,8192]{1,0:T(8,128)(2,1)S(1)} %bitcast.14, bf16[8,2,2,128,256]{4,3,2,1,0:T(8,128)(2,1)S(1)} %get-tuple-element.6.fg, f32[32,256]{1,0:T(8,128)S(1)} %reshape.9.gain), custom_call_target="tpu_custom_call" | custom-call | tf_op jit(solution)/shard_map/finish/pallas_call | solution.py:460
  80.6 0.6 multiply_bitcast_fusion.1
  81.2 0.6 multiply_bitcast_fusion
Async XLA Ops:
  0.6 76.8 %copy-start = (bf16[1,128,8192]{2,1,0:T(8,128)(2,1)S(1)}, bf16[1,128,8192]{2,1,0:T(8,128)(2,1)}, u32[]{:S(2)}) copy-start(bf16[1,128,8192]{2,1,0:T(8,128)(2,1)} %param.6) | copy-start | bytes 6291460
  3.3 1.0 %copy-start.1 = (bf16[1,128,1024]{2,1,0:T(8,128)(2,1)S(1)}, bf16[1,128,1024]{2,1,0:T(8,128)(2,1)}, u32[]{:S(2)}) copy-start(bf16[1,128,1024]{2,1,0:T(8,128)(2,1)} %param.7) | copy-start | bytes 786436
  4.3 0.9 %copy-start.2 = (bf16[1,64,1024]{2,1,0:T(8,128)(2,1)S(1)}, bf16[1,64,1024]{2,1,0:T(8,128)(2,1)}, u32[]{:S(2)}) copy-start(bf16[1,64,1024]{2,1,0:T(8,128)(2,1)} %param.10) | copy-start | bytes 393220

commit v2 on v0

v2 whole, which is shorter than its diff:
```python
import functools
import math

import jax
import jax.numpy as jnp
from jax import lax
from jax.experimental import pallas as pl
from jax.experimental.pallas import tpu as pltpu
from jax.sharding import PartitionSpec as P

adapter_scale = 4.0
gradient_scale = 1.0
norm_eps = 1e-05

F32 = jnp.float32
BF16 = jnp.bfloat16
MESH = pl.DeviceIdType.MESH
ZL, ZH, NX, NY = 8, 2, 4, 4
NZ = ZL * ZH
D = 8192
KV = 1024
R = 64
T = 128
B = 256
NN = (((1,), (0,)), ((), ()))
NT = (((1,), (1,)), ((), ()))
TN = (((0,), (0,)), ((), ()))


def dot(a, b, dims):
    return lax.dot_general(a, b, dims, preferred_element_type=F32)


def mod(a, n):
    return lax.rem(a + 4 * n, n)


def main_kernel(
    x_hbm, grads_hbm, w_hbm, d_hbm, up_hbm, gain_hbm,
    fg, down_out, up_out,
    xv, raw, up, up2, gain, scaled, buf, dbuf, tok, lr4, res, inv,
    part, part_in, summed, chain, lin, upart, upart_in, usum, uin,
    down, upg, s_loc, s_send, r_one, r_z, r_z8, r_dz, r_y1, r_y2, r_sib, r_d, r_p, r_c, r_res,
):
    m = lax.axis_index("member")
    t = lax.axis_index("tensor")
    zh, y, c = m // 8, (m // 2) % 4, m % 2
    zl, xx = t // 4, t % 4
    z = zh * ZL + zl
    par, xs = xx % 2, xx // 2

    def dev(z_, y_, x_, c_):
        return ((z_ // ZL) * 8 + y_ * 2 + c_, (z_ % ZL) * 4 + x_)

    y_up, y_down, y_far = mod(y + 1, NY), mod(y - 1, NY), mod(y + 2, NY)
    zp, zm = dev(mod(z + 1, NZ), y, xx, c), dev(mod(z - 1, NZ), y, xx, c)
    yp, ym, yf = dev(z, y_up, xx, c), dev(z, y_down, xx, c), dev(z, y_far, xx, c)
    sib = dev(z, y, xx, 1 - c)
    xpeer = {d: dev(z, y, mod(xx + d, NX), c) for d in (1, 2, 3)}

    (w2, g_, z_, y1, y2, sb, d_, p_, res_, u_, uz, own_, dz0, dz1, c0, c1) = [
        s_send.at[i] for i in range(16)
    ]
    r_w2, r_g, r_u, r_uz = [r_one.at[i] for i in range(4)]

    def remote(src, dst, sent, got, target):
        return pltpu.make_async_remote_copy(
            src_ref=src, dst_ref=dst, send_sem=sent, recv_sem=got,
            device_id=target, device_id_type=MESH,
        )

    def start(src, dst, sent, got, target):
        remote(src, dst, sent, got, target).start()

    def arrived(ref, got):
        remote(ref, ref, got, got, sib).wait_recv()

    def drained(ref, sent):
        remote(ref, ref, sent, sent, sib).wait_send()

    barrier = pltpu.get_barrier_semaphore()
    for peer in (zp, zm, yp, ym, yf, *xpeer.values(), sib):
        pl.semaphore_signal(barrier, inc=1, device_id=peer, device_id_type=MESH)

    own = buf.at[0, xs, c, y]
    half = KV // 2
    loads = [
        pltpu.make_async_copy(src, dst, s_loc.at[i])
        for i, (src, dst) in enumerate((
            (w_hbm, own),
            (d_hbm, dbuf.at[zl, xx]),
            (grads_hbm, raw),
            (up_hbm, up),
            (x_hbm, xv),
            (gain_hbm, gain),
        ))
    ]
    for cp in loads:
        cp.start()

    def pieces(s):
        return pl.ds(0, 1) if s == 0 else (pl.ds(15, 1) if s == 8 else pl.ds(2 * s - 1, 2))

    def z_slot(s, direction):
        return 0 if s == 0 else (15 if s == 8 else 2 * s - 1 + direction)

    def z_send(s, direction, kind, part):
        start(
            buf.at[z_slot(s - 1, direction), part, c, y],
            buf.at[z_slot(s, direction), part, c, y],
            z_, r_z.at[direction, s, kind], zm if direction else zp,
        )

    def z_step(s, kind):
        half_ = xs if kind == 0 else 1 - xs
        for direction in (0, 1):
            arrived(buf.at[z_slot(s, direction), half_, c, y], r_z.at[direction, s, kind])
            if s < 7:
                z_send(s + 1, direction, kind, half_)
            else:
                pl.when(half_ == direction)(functools.partial(far_copy(direction).start))

    def far_copy(direction):
        return remote(
            buf.at[z_slot(7, direction), direction, c, y], buf.at[15, direction, c, y],
            z_, r_z8.at[direction], zm if direction else zp,
        )

    def in_line(s, direction):
        return zl >= s if direction == 0 else zl + s < ZL

    def more(direction):
        return zl < ZL - 1 if direction == 0 else zl > 0

    def d_copy(s, direction, row):
        ref = dbuf.at[row, xx]
        sent = dz1 if direction else dz0
        return remote(ref, ref, sent, r_dz.at[direction, s], zm if direction else zp)

    def d_pair(s, direction):
        row = zl - s if direction == 0 else zl + s
        ok = in_line(s, direction) & (row % 2 == direction)
        return ok, row // 2

    def d_across(g):
        for d in (1, 2, 3):
            ref = dbuf.at[pl.ds(2 * g, 2), xx]
            start(ref, ref, d_, r_d.at[g], xpeer[d])

    def d_step(s):
        for direction in (0, 1):

            def go(direction=direction):
                row = zl - s if direction == 0 else zl + s
                arrived(dbuf.at[row, xx], r_dz.at[direction, s])

                def forward():
                    d_copy(s, direction, row).wait_send()
                    if s < 7:
                        d_copy(s + 1, direction, row).start()

                pl.when(more(direction))(forward)

            pl.when(in_line(s, direction))(go)
            pl.when((zl == (s - 1 if direction == 0 else 8 - s)) & more(direction))(
                lambda: d_copy(s, direction, zl).wait_send()
            )
            ok, g = d_pair(s, direction)
            pl.when(ok)(functools.partial(d_across, g))

    def d_done(s):
        for direction in (0, 1):
            ok, g = d_pair(s, direction)

            def go(g=g):
                arrived(dbuf.at[pl.ds(2 * g, 2), 0:3], r_d.at[g])

                def add(i, acc):
                    row = 2 * g + i // 4
                    return acc + dot(scaled[8 * g + i], dbuf[row, i % 4], NT)

                lin[...] += lax.fori_loop(0, 8, add, jnp.zeros((T, R), F32), unroll=8)

            pl.when(ok)(go)

    both = pl.ds(0, 2)
    direct_from = 8

    def y_send(s):
        src = buf.at[pieces(s), both, c, y]
        for peer in (yp, ym, yf) if s >= direct_from else (yp, ym):
            start(src, src, y1, r_y1.at[s], peer)

    def y_relay(s):
        arrived(buf.at[pieces(s), both, c, 0:2], r_y1.at[s])
        for direction, near, peer in ((0, y_down, yp), (1, y_up, ym)):
            src = buf.at[pieces(s), direction, c, near]
            start(src, src, y2, r_y2.at[s], peer)

    def y_done(s):
        if s >= direct_from:
            arrived(buf.at[pieces(s), both, c, 0:3], r_y1.at[s])
        else:
            arrived(buf.at[pieces(s), both, c, 0], r_y2.at[s])
        src = buf.at[pieces(s), both, c]
        start(src, src, sb, r_sib.at[s], sib)

    def sib_done(s):
        arrived(buf.at[pieces(s), both, 1 - c], r_sib.at[s])
        if s == 4:
            block(mod(zl + 4, ZL), 8, 7)
        elif s == 8:
            block(zl, 15, 0)
        elif s > 4:
            block(mod(zl + s, ZL), 2 * s, 15 - 2 * s)
            block(mod(zl - s, ZL), 2 * s - 1, 16 - 2 * s)

    def p_pairs(k):
        g = zl // 2
        if k == 4:
            return [(g >= 0, g)]
        return [(g + 4 - k < 4, g + 4 - k), (g - 4 + k >= 0, g - 4 + k)]

    def p_copy(d, g):
        return remote(
            part.at[mod(xx + d, NX), pl.ds(2 * g, 2)], part_in.at[d, pl.ds(2 * g, 2)],
            p_, r_p.at[g], xpeer[d],
        )

    def p_send(k):
        for ok, g in p_pairs(k):

            def go(g=g):
                def one(i, carry):
                    term = dot(lr_t, scaled[8 * g + i], NN)
                    part[i % 4, 2 * g + i // 4] = term.astype(BF16)
                    return carry

                lax.fori_loop(0, 8, one, 0, unroll=8)
                for d in (1, 2, 3):
                    p_copy(d, g).start()

            pl.when(ok)(go)

    def p_done(k):
        for ok, g in p_pairs(k):

            def go(g=g):
                arrived(part_in.at[1:4, pl.ds(2 * g, 2)], r_p.at[g])
                for i in (0, 1):
                    acc = part[xx, 2 * g + i].astype(F32)
                    for d in (1, 2, 3):
                        acc += part_in[d, 2 * g + i].astype(F32)
                    summed[2 * g + i] = acc

            pl.when(ok)(go)

    def c_copy(src, direction, j):
        return remote(
            src, chain.at[direction, j], c1 if direction else c0, r_c.at[direction, j],
            zm if direction else zp,
        )

    def c_step(j):
        for direction, place, row in ((0, zl, zl + 8 - j), (1, 7 - zl, zl - 8 + j)):

            def first(direction=direction, row=row):
                if j > 1:
                    c_copy(summed.at[0], direction, j - 1).wait_send()
                c_copy(summed.at[row], direction, j).start()

            pl.when(place == 0)(first)

            def later(direction=direction, place=place, row=row):
                here = chain.at[direction, j - 1]
                arrived(here, r_c.at[direction, j - 1])
                here[...] += summed[row]
                if j > 2:

                    @pl.when(place <= j - 2)
                    def _():
                        c_copy(here, direction, j - 1).wait_send()

                c_copy(here, direction, j).start()

            if j >= 2:
                pl.when((place >= 1) & (place <= j - 1))(later)

    def c_last():
        down[...] = summed[zl]
        for direction, place in ((0, zl), (1, 7 - zl)):

            def go(direction=direction):
                arrived(chain.at[direction, 7], r_c.at[direction, 7])
                down[...] += chain[direction, 7]

            pl.when(place >= 1)(go)
            pl.when(place <= 6)(
                functools.partial(c_copy(summed.at[0], direction, 7).wait_send)
            )
        pltpu.make_async_copy(down, down_out, s_loc.at[0]).start()

    def res_copy(n, row, p):
        tokens = pl.ds(64 * n, 64)
        return remote(
            res.at[row, :, pl.ds(T + 64 * n, 64)], fg.at[row, :, p, tokens], res_, r_res.at[row],
            xpeer[1 if n else 3],
        )

    def own_copy(row):
        return pltpu.make_async_copy(
            res.at[row, :, 0:T], fg.at[row, :, par], own_
        )

    def block(row, qa, qb):
        steps = (qa + 1) // 2
        first = (mod(z - steps, NZ) if qa % 2 else mod(z + steps, NZ)) // ZL

        def one(i, carry):
            acc = dot(tok[first], buf[qa, i].reshape(half, B), NN)
            acc += dot(tok[1 - first], buf[qb, i].reshape(half, B), NN)
            acc += dot(lr4[...], dbuf[row, par + 2 * i], NN)
            res[row, i] = acc.astype(BF16)
            return carry

        lax.fori_loop(0, 2, one, 0, unroll=2)
        for n in (0, 1):
            res_copy(n, row, par).start()
        own_copy(row).start()

    def core_major(values, h):
        blocks = [values[:, h * half + i * R:h * half + (i + 1) * R] for i in range(8)]
        return jnp.concatenate(blocks[0::2] + blocks[1::2], axis=1)

    def lowrank(rows):
        return (
            dot(tok[0, rows], up2[0], NT) + dot(tok[1, rows], up2[1], NT)
        ).astype(BF16)

    def pack_up():
        lb = lin[...].astype(BF16)
        for h in (0, 1):
            term = dot(tok[h, 0:T], lb, TN)
            term = term.reshape(2, NY, 2, 32, R).swapaxes(1, 2)
            upart[:, 4 * h:4 * h + 4] = term.reshape(NX, 4, 32, R).astype(BF16)
        for d in (1, 2, 3):
            start(upart.at[mod(xx + d, NX)], upart_in.at[d], u_, r_u, xpeer[d])

    def up_over_z():
        acc = upart[xx].astype(F32)
        arrived(upart_in.at[1:4], r_u)
        for d in (1, 2, 3):
            acc += upart_in[d].astype(F32)
        usum[...] = acc
        for d in (4, 3, 5, 2, 6, 1, 7):
            row = mod(zl + d, ZL)
            start(usum.at[row], uin.at[d], uz, r_uz, dev(zh * ZL + row, y, xx, c))

    def up_last():
        acc = usum[zl]
        arrived(uin.at[1:8], r_uz)
        for d in range(1, 8):
            acc += uin[d]
        upg[...] = acc
        pltpu.make_async_copy(upg, up_out, s_loc.at[1]).start()

    def square(i, acc):
        v = xv[:, pl.ds(pl.multiple_of(i * B, B), B)].astype(F32)
        return acc + v * v

    def make_scaled(i, carry):
        columns = pl.ds(pl.multiple_of(i * B, B), B)
        scaled[i] = (xv[:, columns].astype(F32) * inv[...] * gain[:, columns]).astype(BF16)
        return carry

    for i in (0, 1):
        loads[i].wait()
    pl.semaphore_wait(barrier, 9)

    start(own, own, w2, r_w2, xpeer[2])
    for direction in (0, 1):
        z_send(1, direction, 0, xs)
    for direction in (0, 1):
        pl.when(more(direction))(functools.partial(d_copy(1, direction, zl).start))
    loads[2].wait()
    for h in (0, 1):
        tok[h, 0:T] = core_major(raw[...], h)
    for n in (0, 1):
        start(
            tok.at[:, 64 * n:64 * n + 64], tok.at[:, T + 64 * n:T + 64 * n + 64],
            g_, r_g, xpeer[3 if n else 1],
        )
    loads[4].wait()
    total = lax.fori_loop(0, 32, square, jnp.zeros((T, B), F32), unroll=2)
    inv[...] = lax.rsqrt(jnp.sum(total, axis=1, keepdims=True) / D + norm_eps)

    arrived(buf.at[0, 1 - xs, c, y], r_w2)
    for direction in (0, 1):
        z_send(1, direction, 1, 1 - xs)
    y_send(0)

    loads[3].wait()
    for h in (0, 1):
        up2[h] = core_major(up[...], h)
    lr_t = (dot(up2[0], tok[0, 0:T], NT) + dot(up2[1], tok[1, 0:T], NT)).astype(BF16)
    lr4[0:T] = lowrank(slice(0, T)) * adapter_scale
    lin[...] = jnp.zeros_like(lin)
    loads[5].wait()
    lax.fori_loop(0, 32, make_scaled, 0, unroll=2)
    p_send(1)

    d_at = {1: (1,), 2: (2,), 3: (3,), 4: (4,), 5: (5, 6), 6: (7,)}
    d_done_at = {3: (1,), 4: (2,), 5: (3,), 6: (4, 5), 7: (6, 7)}
    for s in range(1, 9):
        if s <= 7:
            z_step(s, 0)
            z_step(s, 1)
        else:
            for direction in (0, 1):
                arrived(buf.at[15, direction, c, y], r_z8.at[direction])
        y_send(s)
        for v in d_at.get(s, ()):
            d_step(v)
        y_relay(s - 1)
        if s >= 2:
            y_done(s - 2)
        if s >= 3:
            sib_done(s - 3)
        if s == 1:
            arrived(tok.at[:, T:2 * T], r_g)
            lr4[T:] = lowrank(slice(T, 2 * T)) * adapter_scale
        if s in (1, 3, 5):
            p_send((s + 3) // 2)
        if s % 2 == 0 and s < 8:
            p_done(s // 2)
        if 2 <= s < 8:
            c_step(s - 1)
        for v in d_done_at.get(s, ()):
            d_done(v)
        if s == 7:
            pack_up()

    y_done(7)
    y_done(8)
    up_over_z()
    sib_done(6)
    p_done(4)
    c_step(7)
    sib_done(7)
    sib_done(8)
    c_last()
    up_last()
    with jax.named_scope("features_wait"):
        for row in range(ZL):
            arrived(fg.at[row, :, 1 - par], r_res.at[row])
    with jax.named_scope("sends_wait"):
        drained(own, w2)
        drained(tok.at[:, 0:T], g_)
        drained(buf.at[0:15, 0, 0, 0:2], z_)
        drained(buf.at[0:11, 0:2, 0, 0:3], y1)
        drained(buf.at[0:15, 0, 0, 0:2], y2)
        drained(buf.at[0:16, 0:2, 0], sb)
        drained(dbuf.at[:, 0:3], d_)
        drained(part.at[0:3], p_)
        drained(res.at[:, 0:1], res_)
        drained(upart.at[1:4], u_)
        drained(usum.at[1:8], uz)
        pltpu.make_async_copy(res.at[:, :, 0:T], fg.at[:, :, par], own_).wait()
        pltpu.make_async_copy(down, down_out, s_loc.at[0]).wait()
        pltpu.make_async_copy(upg, up_out, s_loc.at[1]).wait()


def exchange(x, grads, w, d, up, gain):
    sem = pltpu.SemaphoreType.DMA
    hbm = pl.BlockSpec(memory_space=pl.ANY)
    return pl.pallas_call(
        main_kernel,
        out_shape=(
            jax.ShapeDtypeStruct((ZL, 2, 2, T, B), BF16),
            jax.ShapeDtypeStruct((R, B), F32),
            jax.ShapeDtypeStruct((32, R), F32),
        ),
        in_specs=[hbm] * 6,
        out_specs=(hbm, hbm, hbm),
        scratch_shapes=[
            pltpu.VMEM((T, D), BF16),
            pltpu.VMEM((T, KV), BF16),
            pltpu.VMEM((R, KV), BF16),
            pltpu.VMEM((2, R, KV // 2), BF16),
            pltpu.VMEM((1, D), F32),
            pltpu.VMEM((32, T, B), BF16),
            pltpu.VMEM((16, 2, 2, NY, R, B), BF16),
            pltpu.VMEM((ZL, NX, R, B), BF16),
            pltpu.VMEM((2, 2 * T, KV // 2), BF16),
            pltpu.VMEM((2 * T, R), BF16),
            pltpu.VMEM((ZL, 2, 2 * T, B), BF16),
            pltpu.VMEM((T, 1), F32),
            pltpu.VMEM((NX, ZL, R, B), BF16),
            pltpu.VMEM((NX, ZL, R, B), BF16),
            pltpu.VMEM((ZL, R, B), F32),
            pltpu.VMEM((2, 8, R, B), F32),
            pltpu.VMEM((T, R), F32),
            pltpu.VMEM((NX, ZL, 32, R), BF16),
            pltpu.VMEM((NX, ZL, 32, R), BF16),
            pltpu.VMEM((ZL, 32, R), F32),
            pltpu.VMEM((ZL, 32, R), F32),
            pltpu.VMEM((R, B), F32),
            pltpu.VMEM((32, R), F32),
            sem((6,)),
            sem((16,)),
            sem((4,)),
            sem((2, 8, 2)),
            sem((2,)),
            sem((2, 8)),
            sem((9,)),
            sem((9,)),
            sem((9,)),
            sem((4,)),
            sem((4,)),
            sem((2, 8)),
            sem((8,)),
        ],
        compiler_params=pltpu.CompilerParams(
            collective_id=1, has_side_effects=True, vmem_limit_bytes=60 << 20
        ),
        name="exchange",
    )(x, grads, w, d, up, gain)


def finish_kernel(scaling, x, fg, gain, down, up, out, down_out, up_out):
    @pl.when(pl.program_id(0) == 0)
    def _():
        down_out[...] = scaling * down[...]
        up_out[...] = scaling * up[...]

    rows = x.shape[0]
    squares = jnp.zeros((rows, B), F32)
    products = jnp.zeros((rows, B), F32)
    for i in range(32):
        v = x[:, i * B:(i + 1) * B].astype(F32)
        g = fg[i // 4, (i % 4) // 2, i % 2].astype(F32) * gain[:, i * B:(i + 1) * B]
        squares += v * v
        products += v * g
    inv = lax.rsqrt(jnp.sum(squares, axis=1, keepdims=True) / D + norm_eps)
    slope = inv * inv * (jnp.sum(products, axis=1, keepdims=True) / D)
    for i in range(32):
        v = x[:, i * B:(i + 1) * B].astype(F32)
        g = fg[i // 4, (i % 4) // 2, i % 2].astype(F32) * gain[:, i * B:(i + 1) * B]
        out[:, i * B:(i + 1) * B] = (inv * (g - v * slope)).astype(BF16)


def finish(x, fg, gain, down, up, scaling):
    rows = 64

    def whole(*shape):
        return pl.BlockSpec(shape, lambda i: (0,) * len(shape))

    return pl.pallas_call(
        functools.partial(finish_kernel, scaling),
        grid=(T // rows,),
        out_shape=(
            jax.ShapeDtypeStruct((T, D), BF16),
            jax.ShapeDtypeStruct((R, B), F32),
            jax.ShapeDtypeStruct((32, R), F32),
        ),
        in_specs=[
            pl.BlockSpec((rows, D), lambda i: (i, 0)),
            pl.BlockSpec((ZL, 2, 2, rows, B), lambda i: (0, 0, 0, i, 0)),
            whole(1, D), whole(R, B), whole(32, R),
        ],
        out_specs=(pl.BlockSpec((rows, D), lambda i: (i, 0)), whole(R, B), whole(32, R)),
        compiler_params=pltpu.CompilerParams(vmem_limit_bytes=60 << 20),
        name="finish",
    )(x, fg, gain, down, up)


def per_device(layer_input, value_grads, value_weight, adapter_down, adapter_up, norm_gain):
    scaling = gradient_scale / math.sqrt(layer_input.shape[1] * lax.axis_size("tensor"))
    gain = norm_gain.reshape(1, D)
    fg, down_t, up_t = exchange(
        layer_input[0], value_grads[0], value_weight.T, adapter_down[0].T, adapter_up[0], gain
    )
    input_grads, down_grads, up_grads = finish(
        layer_input[0], fg, gain, down_t, up_t, scaling
    )
    return (input_grads[None], down_grads.T[None], up_grads.T[None])


def solution(mesh):
    return jax.shard_map(
        per_device,
        mesh=mesh,
        in_specs=(
            P("member", "tensor", None),
            P("member", "tensor", None),
            P("tensor", "member"),
            P("member", "tensor", None),
            P("member", None, None),
            P(),
        ),
        out_specs=(
            P("member", "tensor", None),
            P("member", "tensor", None),
            P("member", None, "tensor"),
        ),
        check_vma=False,
    )
```

time: 957 us -> 71.4 us (0.07)
  the two profiles are of different devices: /device:TPU:8 before, /device:TPU:1 now
where the time goes in v2:
time: 71.4 us; the launch traced here: 71.2 us
  Pallas kernels  70.6 us (99%)
    pallas_call x1, Pallas kernels, exchange(): pl.pallas_call(main_kernel, out_shape=(jax.ShapeDtypeStruct((ZL, 2, 2, T,...  66.3 us
    pallas_call x1, Pallas kernels, finish(): pl.pallas_call(functools.partial(finish_kernel, scaling), grid=(T // rows...  4.35 us

profile of v2, /device:TPU:1, one launch (start us, length us, event | category | flops | bytes accessed | tf_op | source)
XLA Modules:
  0.0 71.2 jit_solution(12486318081873601007)
XLA Ops:
  0.6 66.3 %exchange.1 = (bf16[8,2,2,128,256]{4,3,2,1,0:T(8,128)(2,1)}, f32[64,256]{1,0:T(8,128)}, f32[32,64]{1,0:T(8,128)}) custom-call(bf16[128,8192]{1,0:T(8,128)(2,1)} %bitcast.15, bf16[128,1024]{1,0:T(8,128)(2,1)} %bitcast.17, bf16[64,256]{1,0:T(8,128)(2,1)} %bitcast.21, bf16[64,256]{1,0:T(8,128)(2,1)} %bitcast.22, bf16[64,1024]{1,0:T(8,128)(2,1)} %bitcast.20, ...), custom_call_target="tpu_custom_call" | custom-call | tf_op jit(solution)/shard_map/exchange/pallas_call | solution.py:476
  66.9 4.3 %finish.1 = (bf16[128,8192]{1,0:T(8,128)(2,1)}, f32[64,256]{1,0:T(8,128)}, f32[32,64]{1,0:T(8,128)}) custom-call(bf16[128,8192]{1,0:T(8,128)(2,1)} %bitcast.16, bf16[8,2,2,128,256]{4,3,2,1,0:T(8,128)(2,1)} %get-tuple-element.9.fg, f32[1,8192]{1,0:T(1,128)} %bitcast.19, f32[64,256]{1,0:T(8,128)} %get-tuple-element.10.down, f32[32,64]{1,0:T(8,128)} %get-tuple-element.11.up), custom_call_target="tpu_custom_call" | custom-call | tf_op jit(solution)/shard_map/finish/pallas_call | solution.py:558

commit v3 on v2

--- a/solution.py
+++ b/solution.py
@@ -40,7 +40,7 @@
     fg, down_out, up_out,
     xv, raw, up, up2, gain, scaled, buf, dbuf, tok, lr4, res, inv,
     part, part_in, summed, chain, lin, upart, upart_in, usum, uin,
-    down, upg, s_loc, s_send, r_one, r_z, r_z8, r_dz, r_y1, r_y2, r_sib, r_d, r_p, r_c, r_res,
+    down, upg, s_loc, s_send, r_yz, r_one, r_z, r_z8, r_dz, r_y1, r_y2, r_sib, r_d, r_p, r_c, r_res,
 ):
     m = lax.axis_index("member")
     t = lax.axis_index("tensor")
@@ -58,8 +58,8 @@
     sib = dev(z, y, xx, 1 - c)
     xpeer = {d: dev(z, y, mod(xx + d, NX), c) for d in (1, 2, 3)}
 
-    (w2, g_, z_, y1, y2, sb, d_, p_, res_, u_, uz, own_, dz0, dz1, c0, c1) = [
-        s_send.at[i] for i in range(16)
+    (w2, g_, z_, y1, y2, yz, sb, d_, p_, res_, u_, uz, own_, dz0, dz1, c0, c1) = [
+        s_send.at[i] for i in range(17)
     ]
     r_w2, r_g, r_u, r_uz = [r_one.at[i] for i in range(4)]
 
@@ -79,7 +79,7 @@
         remote(ref, ref, sent, sent, sib).wait_send()
 
     barrier = pltpu.get_barrier_semaphore()
-    for peer in (zp, zm, yp, ym, yf, *xpeer.values(), sib):
+    for peer in (zp, zm, yp, ym, *xpeer.values(), sib):
         pl.semaphore_signal(barrier, inc=1, device_id=peer, device_id_type=MESH)
 
     own = buf.at[0, xs, c, y]
@@ -184,22 +184,38 @@
             pl.when(ok)(go)
 
     both = pl.ds(0, 2)
-    direct_from = 8
-
-    def y_send(s):
-        src = buf.at[pieces(s), both, c, y]
-        for peer in (yp, ym, yf) if s >= direct_from else (yp, ym):
-            start(src, src, y1, r_y1.at[s], peer)
-
-    def y_relay(s):
-        arrived(buf.at[pieces(s), both, c, 0:2], r_y1.at[s])
-        for direction, near, peer in ((0, y_down, yp), (1, y_up, ym)):
-            src = buf.at[pieces(s), direction, c, near]
-            start(src, src, y2, r_y2.at[s], peer)
+    halves = (xs, 1 - xs)
+
+    def y_send(s, kind):
+        src = buf.at[pieces(s), halves[kind], c, y]
+        for peer in (yp, ym):
+            start(src, src, y1, r_y1.at[s, kind], peer)
+
+    def y_send_far():
+        src = buf.at[pieces(8), both, c, y]
+        for peer in (yp, ym, yf):
+            start(src, src, y2, r_y1.at[8, 0], peer)
+
+    def z_whole(k):
+        other = mod(y + k, NY)
+        for direction, peer in ((0, zp), (1, zm)):
+            start(
+                buf.at[0, both, c, other], buf.at[1 + direction, both, c, other],
+                yz, r_yz.at[direction], peer,
+            )
+
+    def y_relay(s, kind):
+        half_ = halves[kind]
+        arrived(buf.at[pieces(s), half_, c, 0:2], r_y1.at[s, kind])
+        src = buf.at[pieces(s), half_, c, mod(y - 1 + 2 * half_, NY)]
+        start(src, src, y2, r_y2.at[s], dev(z, mod(y + 1 - 2 * half_, NY), xx, c))
 
     def y_done(s):
-        if s >= direct_from:
-            arrived(buf.at[pieces(s), both, c, 0:3], r_y1.at[s])
+        if s == 8:
+            arrived(buf.at[pieces(s), both, c, 0:3], r_y1.at[s, 0])
+        elif s == 1:
+            for direction in (0, 1):
+                arrived(buf.at[1 + direction, both, c, 0:3], r_yz.at[direction])
         else:
             arrived(buf.at[pieces(s), both, c, 0], r_y2.at[s])
         src = buf.at[pieces(s), both, c]
@@ -375,11 +391,12 @@
 
     for i in (0, 1):
         loads[i].wait()
-    pl.semaphore_wait(barrier, 9)
+    pl.semaphore_wait(barrier, 8)
 
     start(own, own, w2, r_w2, xpeer[2])
     for direction in (0, 1):
         z_send(1, direction, 0, xs)
+    y_send(0, 0)
     for direction in (0, 1):
         pl.when(more(direction))(functools.partial(d_copy(1, direction, zl).start))
     loads[2].wait()
@@ -397,7 +414,7 @@
     arrived(buf.at[0, 1 - xs, c, y], r_w2)
     for direction in (0, 1):
         z_send(1, direction, 1, 1 - xs)
-    y_send(0)
+    y_send(0, 1)
 
     loads[3].wait()
     for h in (0, 1):
@@ -409,44 +426,60 @@
     lax.fori_loop(0, 32, make_scaled, 0, unroll=2)
     p_send(1)
 
-    d_at = {1: (1,), 2: (2,), 3: (3,), 4: (4,), 5: (5, 6), 6: (7,)}
-    d_done_at = {3: (1,), 4: (2,), 5: (3,), 6: (4, 5), 7: (6, 7)}
-    for s in range(1, 9):
-        if s <= 7:
-            z_step(s, 0)
-            z_step(s, 1)
-        else:
-            for direction in (0, 1):
-                arrived(buf.at[15, direction, c, y], r_z8.at[direction])
-        y_send(s)
-        for v in d_at.get(s, ()):
-            d_step(v)
-        y_relay(s - 1)
-        if s >= 2:
-            y_done(s - 2)
-        if s >= 3:
-            sib_done(s - 3)
+    d_done_at = {3: (1,), 4: (2,), 5: (3,), 6: (4,), 7: (5,)}
+    p_done_at = {3: 1, 5: 2, 7: 3}
+    y_done_at = {2: (0,), 5: (1, 2), 6: (3, 4), 7: (5,)}
+    for s in range(1, 8):
+        for kind in (0, 1):
+            z_step(s, kind)
+            if s > 1:
+                y_send(s, kind)
+        if s != 2:
+            y_relay(s - 1, 0)
+            y_relay(s - 1, 1)
+        if s <= 6:
+            d_step(s)
+        for v in y_done_at.get(s, ()):
+            y_done(v)
+        if 2 <= s <= 4:
+            z_whole(s - 1)
         if s == 1:
             arrived(tok.at[:, T:2 * T], r_g)
             lr4[T:] = lowrank(slice(T, 2 * T)) * adapter_scale
         if s in (1, 3, 5):
             p_send((s + 3) // 2)
-        if s % 2 == 0 and s < 8:
-            p_done(s // 2)
-        if 2 <= s < 8:
-            c_step(s - 1)
+        if s in p_done_at:
+            p_done(p_done_at[s])
+        if s >= 3:
+            c_step(s - 2)
         for v in d_done_at.get(s, ()):
             d_done(v)
-        if s == 7:
-            pack_up()
-
+        if s == 6:
+            d_step(7)
+
+    y_relay(7, 0)
+    y_relay(7, 1)
+    for direction in (0, 1):
+        arrived(buf.at[15, direction, c, y], r_z8.at[direction])
+    y_send_far()
+    y_done(6)
+    c_step(6)
+    p_done(4)
+    d_done(6)
+    d_done(7)
+    pack_up()
+    sib_done(4)
+    sib_done(3)
+    sib_done(5)
     y_done(7)
     y_done(8)
     up_over_z()
+    sib_done(2)
     sib_done(6)
-    p_done(4)
     c_step(7)
+    sib_done(1)
     sib_done(7)
+    sib_done(0)
     sib_done(8)
     c_last()
     up_last()
@@ -457,8 +490,9 @@
         drained(own, w2)
         drained(tok.at[:, 0:T], g_)
         drained(buf.at[0:15, 0, 0, 0:2], z_)
-        drained(buf.at[0:11, 0:2, 0, 0:3], y1)
-        drained(buf.at[0:15, 0, 0, 0:2], y2)
+        drained(buf.at[0:13, 0, 0], y1)
+        drained(buf.at[0:16, 0, 0, 0:2], y2)
+        drained(buf.at[0:3, 0, 0], yz)
         drained(buf.at[0:16, 0:2, 0], sb)
         drained(dbuf.at[:, 0:3], d_)
         drained(part.at[0:3], p_)
@@ -507,12 +541,13 @@
             pltpu.VMEM((R, B), F32),
             pltpu.VMEM((32, R), F32),
             sem((6,)),
-            sem((16,)),
+            sem((17,)),
+            sem((2,)),
             sem((4,)),
             sem((2, 8, 2)),
             sem((2,)),
             sem((2, 8)),
-            sem((9,)),
+            sem((9, 2)),
             sem((9,)),
             sem((9,)),
             sem((4,)),

time: 71.4 us -> 70.3 us (0.985)
  Pallas kernels: 70.6 us -> 69.6 us
    pallas_call x1, Pallas kernels: 66.3 us -> 65.2 us  [exchange(): pl.pallas_call(main_kernel, out_shape=(jax.ShapeDtypeStruct((ZL, 2, 2, T,...]
where the time goes in v3:
time: 70.3 us; the launch traced here: 70.2 us
  Pallas kernels  69.6 us (99%)
    pallas_call x1, Pallas kernels, exchange(): pl.pallas_call(main_kernel, out_shape=(jax.ShapeDtypeStruct((ZL, 2, 2, T,...  65.2 us
    pallas_call x1, Pallas kernels, finish(): pl.pallas_call(functools.partial(finish_kernel, scaling), grid=(T // rows...  4.35 us

profile of v3, /device:TPU:1, one launch (start us, length us, event | category | flops | bytes accessed | tf_op | source)
XLA Modules:
  0.0 70.2 jit_solution(13140642999936260506)
XLA Ops:
  0.6 65.2 %exchange.1 = (bf16[8,2,2,128,256]{4,3,2,1,0:T(8,128)(2,1)}, f32[64,256]{1,0:T(8,128)}, f32[32,64]{1,0:T(8,128)}) custom-call(bf16[128,8192]{1,0:T(8,128)(2,1)} %bitcast.15, bf16[128,1024]{1,0:T(8,128)(2,1)} %bitcast.17, bf16[64,256]{1,0:T(8,128)(2,1)} %bitcast.21, bf16[64,256]{1,0:T(8,128)(2,1)} %bitcast.22, bf16[64,1024]{1,0:T(8,128)(2,1)} %bitcast.20, ...), custom_call_target="tpu_custom_call" | custom-call | tf_op jit(solution)/shard_map/exchange/pallas_call | solution.py:510
  65.8 4.3 %finish.1 = (bf16[128,8192]{1,0:T(8,128)(2,1)}, f32[64,256]{1,0:T(8,128)}, f32[32,64]{1,0:T(8,128)}) custom-call(bf16[128,8192]{1,0:T(8,128)(2,1)} %bitcast.16, bf16[8,2,2,128,256]{4,3,2,1,0:T(8,128)(2,1)} %get-tuple-element.9.fg, f32[1,8192]{1,0:T(1,128)} %bitcast.19, f32[64,256]{1,0:T(8,128)} %get-tuple-element.10.down, f32[32,64]{1,0:T(8,128)} %get-tuple-element.11.up), custom_call_target="tpu_custom_call" | custom-call | tf_op jit(solution)/shard_map/finish/pallas_call | solution.py:593

commit v4 on v3

--- a/solution.py
+++ b/solution.py
@@ -358,7 +358,7 @@
         for h in (0, 1):
             term = dot(tok[h, 0:T], lb, TN)
             term = term.reshape(2, NY, 2, 32, R).swapaxes(1, 2)
-            upart[:, 4 * h:4 * h + 4] = term.reshape(NX, 4, 32, R).astype(BF16)
+            upart[:, :, :, h * R:(h + 1) * R] = term.reshape(NX, 4, 32, R).astype(BF16)
         for d in (1, 2, 3):
             start(upart.at[mod(xx + d, NX)], upart_in.at[d], u_, r_u, xpeer[d])
 
@@ -367,7 +367,8 @@
         arrived(upart_in.at[1:4], r_u)
         for d in (1, 2, 3):
             acc += upart_in[d].astype(F32)
-        usum[...] = acc
+        for h in (0, 1):
+            usum[4 * h:4 * h + 4] = acc[:, :, h * R:(h + 1) * R]
         for d in (4, 3, 5, 2, 6, 1, 7):
             row = mod(zl + d, ZL)
             start(usum.at[row], uin.at[d], uz, r_uz, dev(zh * ZL + row, y, xx, c))
@@ -534,8 +535,8 @@
             pltpu.VMEM((ZL, R, B), F32),
             pltpu.VMEM((2, 8, R, B), F32),
             pltpu.VMEM((T, R), F32),
-            pltpu.VMEM((NX, ZL, 32, R), BF16),
-            pltpu.VMEM((NX, ZL, 32, R), BF16),
+            pltpu.VMEM((NX, ZL // 2, 32, 2 * R), BF16),
+            pltpu.VMEM((NX, ZL // 2, 32, 2 * R), BF16),
             pltpu.VMEM((ZL, 32, R), F32),
             pltpu.VMEM((ZL, 32, R), F32),
             pltpu.VMEM((R, B), F32),

time: 70.3 us -> 70.2 us (level)
  no operation moved by 1% of the time
where the time goes in v4:
time: 70.2 us; the launch traced here: 70.1 us
  Pallas kernels  69.5 us (99%)
    pallas_call x1, Pallas kernels, exchange(): pl.pallas_call(main_kernel, out_shape=(jax.ShapeDtypeStruct((ZL, 2, 2, T,...  65.1 us
    pallas_call x1, Pallas kernels, finish(): pl.pallas_call(functools.partial(finish_kernel, scaling), grid=(T // rows...  4.35 us

profile of v4, /device:TPU:1, one launch (start us, length us, event | category | flops | bytes accessed | tf_op | source)
XLA Modules:
  0.0 70.1 jit_solution(452597606733434253)
XLA Ops:
  0.6 65.1 %exchange.1 = (bf16[8,2,2,128,256]{4,3,2,1,0:T(8,128)(2,1)}, f32[64,256]{1,0:T(8,128)}, f32[32,64]{1,0:T(8,128)}) custom-call(bf16[128,8192]{1,0:T(8,128)(2,1)} %bitcast.15, bf16[128,1024]{1,0:T(8,128)(2,1)} %bitcast.17, bf16[64,256]{1,0:T(8,128)(2,1)} %bitcast.21, bf16[64,256]{1,0:T(8,128)(2,1)} %bitcast.22, bf16[64,1024]{1,0:T(8,128)(2,1)} %bitcast.20, ...), custom_call_target="tpu_custom_call" | custom-call | tf_op jit(solution)/shard_map/exchange/pallas_call | solution.py:511
  65.8 4.3 %finish.1 = (bf16[128,8192]{1,0:T(8,128)(2,1)}, f32[64,256]{1,0:T(8,128)}, f32[32,64]{1,0:T(8,128)}) custom-call(bf16[128,8192]{1,0:T(8,128)(2,1)} %bitcast.16, bf16[8,2,2,128,256]{4,3,2,1,0:T(8,128)(2,1)} %get-tuple-element.9.fg, f32[1,8192]{1,0:T(1,128)} %bitcast.19, f32[64,256]{1,0:T(8,128)} %get-tuple-element.10.down, f32[32,64]{1,0:T(8,128)} %get-tuple-element.11.up), custom_call_target="tpu_custom_call" | custom-call | tf_op jit(solution)/shard_map/finish/pallas_call | solution.py:594
